TPU v7x, 32 devices: a whole 2x2x4 slice. The times are simulated.
32 devices in a mesh: ctx: 8 (over z, y), head: 4 (over x, core).
Axes of the slice: x: 2, y: 2, z: 4, core: 2. Of those that a mesh axis runs over, the one named last changes fastest.
Arguments:
- delta_q: bfloat16 [2048, 2048], P('ctx', 'head'), may hold values from -6 to 6
- delta_k: bfloat16 [2048, 2048], P('ctx', 'head'), may hold values from -6 to 6
- delta_v: bfloat16 [2048, 2048], P('ctx', 'head'), may hold values from -6 to 6
- beta: float32 [2048, 16], P('ctx', 'head'), may hold values from 0 to 0.9, as said below
- log_decay: float32 [2048, 16], P('ctx', 'head'), may hold values from -1 to 0, as said below
- out_gate: bfloat16 [2048, 2048], P('ctx', 'head'), may hold values from -6 to 6
- norm_gain: float32 [128], replicated, may hold values from 0.1 to 1.9
- attn_q: bfloat16 [2048, 2048], P('ctx', 'head'), may hold values from -16 to 16
- attn_k: bfloat16 [2048, 2048], P('ctx', 'head'), may hold values from -16 to 16
- attn_v: bfloat16 [2048, 2048], P('ctx', 'head'), may hold values from -6 to 6
- w_delta_out: bfloat16 [2048, 2048], P('head'), may hold values from -0.125 to 0.125
- w_attn_out: bfloat16 [2048, 2048], P('head'), may hold values from -0.125 to 0.125
Outputs:
- branch_sum: bfloat16 [2048, 2048], P(('ctx', 'head'))
Inputs may be any that keep to these rules, and one draw needn't show every extreme that they name: `beta`: write strengths, positive. `log_decay`: log decays, negative.
All inputs are finite; a program needn't handle non-finite values.
Results may differ from a plain program's by a relative error of at most 0.022.
Values may be sent and summed in bfloat16 or wider, within the bound.
A program may use at most 128 MiB of HBM per device.

v0:
```python
import jax
import jax.numpy as jnp
from jax import lax
from jax.sharding import PartitionSpec as P

DH = 128
WINDOW = 1024


highest = lax.Precision.HIGHEST


def carried_in(shard, axis, join, neutral):
    place = lax.axis_index(axis)
    gathered = jax.tree.map(
        lambda a, kind: lax.all_gather(a.astype(kind), axis),
        shard,
        jax.tree.map(lambda a: jnp.bfloat16 if a.dtype == jnp.float32 else a.dtype, shard),
    )
    state = jax.tree.map(lambda a, e: jnp.zeros_like(a) + jnp.asarray(e, a.dtype), shard, neutral)

    def one(turn, state):
        return join(
            state,
            jax.tree.map(
                lambda a, own: lax.dynamic_index_in_dim(a, turn, 0, False).astype(own.dtype),
                gathered,
                shard,
            ),
        )

    return lax.fori_loop(0, place, one, state)


def passed_along(block, axis, distance):
    devices = range(lax.axis_size(axis))
    route = [(i - distance, i) for i in devices if i - distance in devices]
    return lax.ppermute(block, axis, route)


def unit_rows(array):
    return array / jnp.sqrt(jnp.sum(array * array, axis=-1, keepdims=True) + 1e-06)


def unit_inverse(lower_part):
    order_len = lower_part.shape[-1]
    identity = jnp.eye(order_len, dtype=jnp.float32)
    powered = -lower_part
    result = identity + powered
    for counter in range(1, max(1, (order_len - 1).bit_length())):
        powered = jnp.matmul(powered, powered, precision=highest)
        result = jnp.matmul(result, identity + powered, precision=highest)
    return result


def block_terms(queries, keys_in, values_in, betas, log_rates):
    cumulative = jnp.cumsum(log_rates, axis=-1)
    length = queries.shape[-2]
    positions = jnp.arange(length)
    strict = positions[:, None] > positions[None, :]
    inclusive = positions[:, None] >= positions[None, :]
    spread = cumulative[..., :, None] - cumulative[..., None, :]
    ratio_strict = jnp.where(strict, jnp.exp(jnp.where(strict, spread, 0.0)), 0.0)
    ratio_incl = jnp.where(inclusive, jnp.exp(jnp.where(inclusive, spread, 0.0)), 0.0)
    key_gram = jnp.einsum("...td,...sd->...ts", keys_in, keys_in, precision=highest)
    inverse = unit_inverse(betas[..., :, None] * ratio_strict * key_gram)
    decayed = jnp.exp(cumulative)
    pseudo = jnp.matmul(inverse, betas[..., None] * values_in, precision=highest)
    writer = jnp.matmul(inverse, (betas * decayed)[..., None] * keys_in, precision=highest)
    to_end = jnp.exp(cumulative[..., -1:] - cumulative)
    keys_end = keys_in * to_end[..., None]
    identity = jnp.eye(queries.shape[-1], dtype=jnp.float32)
    transition = jnp.exp(cumulative[..., -1])[..., None, None] * identity - jnp.einsum(
        "...td,...te->...de", keys_end, writer, precision=highest
    )
    contrib = jnp.einsum("...td,...te->...de", keys_end, pseudo, precision=highest)
    mixing = ratio_incl * jnp.einsum("...td,...sd->...ts", queries, keys_in, precision=highest)
    local_out = jnp.matmul(mixing, pseudo, precision=highest)
    carry_out = decayed[..., None] * queries - jnp.matmul(mixing, writer, precision=highest)
    return (transition, contrib, local_out, carry_out)


def window_block(queries, keys_in, values_in, query_pos, key_pos):
    scores = jnp.einsum(
        "thd,shd->hts", queries, keys_in, preferred_element_type=jnp.float32
    ) * DH ** (-0.5)
    offsets = query_pos[:, None] - key_pos[None, :]
    inside = (offsets >= 0) & (offsets < WINDOW) & (key_pos[None, :] >= 0)
    masked = jnp.where(inside[None], scores, -1e30)
    block_max = jnp.max(masked, axis=-1)
    weights = jnp.where(inside[None], jnp.exp(masked - block_max[..., None]), 0.0)
    probs = weights.astype(jnp.bfloat16)
    block_num = jnp.einsum("hts,shd->htd", probs, values_in, preferred_element_type=jnp.float32)
    block_den = jnp.sum(weights, axis=-1)
    return (block_max, block_num, block_den)


def chain_pairs(earlier, later):
    matrix = jnp.einsum("hij,hjk->hik", later[0], earlier[0], precision=highest)
    vector = jnp.einsum("hij,hjk->hik", later[0], earlier[1], precision=highest) + later[1]
    return (matrix, vector)


def shards(
    delta_q,
    delta_k,
    delta_v,
    beta,
    log_decay,
    out_gate,
    norm_gain,
    attn_q,
    attn_k,
    attn_v,
    w_delta_out,
    w_attn_out,
):
    rows_here = delta_q.shape[0]
    local_heads = delta_q.shape[1] // DH
    block_len = min(64, rows_here)
    blocks = rows_here // block_len

    def heads_blocks(array):
        return (
            array.astype(jnp.float32)
            .reshape(blocks, block_len, local_heads, DH)
            .transpose(2, 0, 1, 3)
        )

    queries = unit_rows(heads_blocks(delta_q)) * DH ** (-0.5)
    keys_in = unit_rows(heads_blocks(delta_k))
    values_in = heads_blocks(delta_v)
    betas = beta.reshape(blocks, block_len, local_heads).transpose(2, 0, 1)
    log_rates = log_decay.reshape(blocks, block_len, local_heads).transpose(2, 0, 1)
    transition, contrib, local_out, carry_out = block_terms(
        queries, keys_in, values_in, betas, log_rates
    )
    identity = jnp.broadcast_to(jnp.eye(DH, dtype=jnp.float32), (local_heads, DH, DH))
    zero_state = jnp.zeros((local_heads, DH, DH), jnp.float32)

    def compose(carried, inputs):
        after_pair = chain_pairs(carried, inputs)
        return (after_pair, carried)

    shard_pair, starts = lax.scan(
        compose,
        (identity, zero_state),
        (transition.transpose(1, 0, 2, 3), contrib.transpose(1, 0, 2, 3)),
    )
    start_mats = starts[0].transpose(1, 0, 2, 3)
    start_vecs = starts[1].transpose(1, 0, 2, 3)
    own_out = local_out + jnp.einsum("hntd,hnde->hnte", carry_out, start_vecs, precision=highest)
    reach = jnp.einsum("hntd,hnde->hnte", carry_out, start_mats, precision=highest)
    prefix_pair = carried_in(shard_pair, "ctx", chain_pairs, (identity, zero_state))
    incoming_state = prefix_pair[1]
    delta_raw = own_out + jnp.einsum("hntd,hde->hnte", reach, incoming_state, precision=highest)
    delta_raw = delta_raw.transpose(1, 2, 0, 3).reshape(rows_here, local_heads, DH)
    gate_act = jax.nn.silu(out_gate.astype(jnp.float32).reshape(rows_here, local_heads, DH))
    normed = (
        delta_raw
        / jnp.sqrt(jnp.mean(delta_raw * delta_raw, axis=-1, keepdims=True) + 1e-06)
        * norm_gain
        * gate_act
    )
    delta_heads = normed.reshape(rows_here, local_heads * DH).astype(jnp.bfloat16)
    position = lax.axis_index("ctx")
    query_rows = attn_q.reshape(rows_here, local_heads, DH)
    query_pos = position * rows_here + jnp.arange(rows_here, dtype=jnp.int32)
    maxima, numers, denoms = ([], [], [])
    own_max, own_num, own_den = window_block(
        query_rows,
        attn_k.reshape(rows_here, local_heads, DH),
        attn_v.reshape(rows_here, local_heads, DH),
        query_pos,
        query_pos,
    )
    maxima.append(own_max)
    numers.append(own_num)
    denoms.append(own_den)
    for back in range(1, WINDOW // rows_here + 1):
        keys_far, values_far = passed_along((attn_k, attn_v), "ctx", back)
        key_pos = (position - back) * rows_here + jnp.arange(rows_here, dtype=jnp.int32)
        remote_maximum, far_num, far_den = window_block(
            query_rows,
            keys_far.reshape(rows_here, local_heads, DH),
            values_far.reshape(rows_here, local_heads, DH),
            query_pos,
            key_pos,
        )
        maxima.append(remote_maximum)
        numers.append(far_num)
        denoms.append(far_den)
    top = maxima[0]
    for block_max in maxima[1:]:
        top = jnp.maximum(top, block_max)
    numer = jnp.zeros_like(numers[0])
    denom = jnp.zeros_like(denoms[0])
    for block_max, block_num, block_den in zip(maxima, numers, denoms):
        factor = jnp.exp(block_max - top)
        numer = numer + factor[..., None] * block_num
        denom = denom + factor * block_den
    attn_heads = (
        (numer / denom[..., None])
        .transpose(1, 0, 2)
        .reshape(rows_here, local_heads * DH)
        .astype(jnp.bfloat16)
    )
    running_partial_sum = jnp.dot(delta_heads, w_delta_out, preferred_element_type=jnp.float32)
    running_partial_sum = running_partial_sum + jnp.dot(
        attn_heads, w_attn_out, preferred_element_type=jnp.float32
    )
    total = lax.psum_scatter(
        running_partial_sum.astype(jnp.bfloat16), "head", scatter_dimension=0, tiled=True
    )
    return total


def solution(mesh):
    return jax.shard_map(
        shards,
        mesh=mesh,
        in_specs=(
            P("ctx", "head"),
            P("ctx", "head"),
            P("ctx", "head"),
            P("ctx", "head"),
            P("ctx", "head"),
            P("ctx", "head"),
            P(),
            P("ctx", "head"),
            P("ctx", "head"),
            P("ctx", "head"),
            P("head", None),
            P("head", None),
        ),
        out_specs=P(("ctx", "head"), None),
        check_vma=False,
    )
```

profile of v0, /device:TPU:17, one launch (start us, length us, event | category | flops | bytes accessed | tf_op | source)
XLA Modules:
  0.0 201.9 jit_solution(2723377550062878074)
XLA Ops:
  6.6 0.9 reshape.492
  7.5 1.1 reshape.510
  8.6 1.3 reshape.511
  10.5 0.9 reduce_window_sum.11
  12.2 0.7 subtract_exponential_fusion
  13.5 1.2 fusion.23
  20.6 1.9 reshape.512
  23.3 2.0 fusion.77
  25.3 0.7 fusion.63
  26.0 3.1 %convolution_bitcast_fusion = f32[4,4,128,128]{3,2,0,1:T(8,128)} fusion(f32[4,4,64,128]{3,2,1,0:T(8,128)S(1)} %fusion.63, f32[4,4,64]{2,1,0:T(4,128)S(1)} %copy-done.32, f32[4,64,4,128]{3,2,1,0:T(4,128)S(1)} %copy-done.13, f32[4,4,64]{2,1,0:T(4,128)S(1)} %copy-done.31), kind=kOutput, calls=%fused_computation.20 | convolution fusion | flops 201588736 | bytes 2105344 | tf_op jit(solution)/shard_map/...td,...te->...de/dot_general | solution.py:76
  29.1 3.3 %fusion.15 = f32[4,4,128,128]{3,2,0,1:T(8,128)} fusion(f32[4,4,64,128]{3,2,1,0:T(8,128)S(1)} %fusion.77, f32[128,128]{1,0:T(8,128)S(1)} %fusion.134, f32[4,4]{0,1:T(4,128)S(1)} %copy-done.36, f32[4,4,64]{2,1,0:T(4,128)S(1)} %copy-done.32, f32[4,64,4,128]{3,2,1,0:T(4,128)S(1)} %copy-done.13, f32[4,4,64]{2,1,0:T(4,128)S(1)} %copy-done.31), kind=kOutput, calls=%fused_computation.22 | convolution fusion | flops 202113024 | bytes 2170944 | tf_op jit(solution)/shard_map/...td,...te->...de/dot_general | solution.py:73
  32.4 14.8 %while.30 = (s32[]{:T(128)}, f32[4,128,128]{2,1,0:T(8,128)S(1)}, f32[4,128,128]{2,1,0:T(8,128)S(1)}, f32[4,4,128,128]{3,2,1,0:T(8,128)}, f32[4,4,128,128]{3,2,1,...) while((s32[]{:T(128)}, f32[4,128,128]{2,1,0:T(8,128)S(1)}, ...), condition=%wide.region_4.5_spmd.clone, body=%wide.region_3.4_spmd.clone.sunk | while | flops 201523200 | bytes 3933815 | solution.py:145
  32.5 0.8 bitcast_dynamic-update-slice_fusion.3
  33.3 1.3 fusion.229
  34.7 1.4 convolution_add_fusion.8
  36.2 0.8 bitcast_dynamic-update-slice_fusion.3
  37.0 1.3 fusion.229
  38.4 1.4 convolution_add_fusion.8
  39.9 0.8 bitcast_dynamic-update-slice_fusion.3
  40.7 1.3 fusion.229
  42.1 1.4 convolution_add_fusion.8
  43.6 0.8 bitcast_dynamic-update-slice_fusion.3
  44.4 1.3 fusion.229
  45.8 1.4 convolution_add_fusion.8
  48.0 1.8 copy.76
  49.8 1.3 collective-permute-start.3
  51.1 3.2 %collective-permute-start.1 = (bf16[256,512]{0,1:T(8,128)(2,1)}, bf16[256,512]{0,1:T(8,128)(2,1)S(1)}, u32[]{:S(2)}, u32[]{:S(2)}) collective-permute-start(bf16[256,512]{0,1:T(8,128)(2,1)} %copy.76), channel_id=1, source_target_pairs={{0,8},{4,12},{8,16},{12,20},{16,24},{20,28},{1,9},{5,13},{9,17},{1... | collective-permute-start | bytes 786440 | tf_op jit(solution)/shard_map/ppermute | solution.py:38
  54.3 2.2 %collective-permute-start.2 = (bf16[256,512]{0,1:T(8,128)(2,1)}, bf16[256,512]{0,1:T(8,128)(2,1)}, u32[]{:S(2)}, u32[]{:S(2)}) collective-permute-start(bf16[256,512]{0,1:T(8,128)(2,1)} %copy.76), channel_id=1, source_target_pairs={{0,12},{4,16},{8,20},{12,24},{16,28},{1,13},{5,17},{9,21},{13,25},... | collective-permute-start | bytes 786440 | tf_op jit(solution)/shard_map/ppermute | solution.py:38
  56.5 2.2 %collective-permute-start = (bf16[256,512]{0,1:T(8,128)(2,1)}, bf16[256,512]{0,1:T(8,128)(2,1)}, u32[]{:S(2)}, u32[]{:S(2)}) collective-permute-start(bf16[256,512]{0,1:T(8,128)(2,1)} %copy.76), channel_id=1, source_target_pairs={{0,4},{4,8},{8,12},{12,16},{16,20},{20,24},{24,28},{1,5},{5,9},{9,... | collective-permute-start | bytes 786440 | tf_op jit(solution)/shard_map/ppermute | solution.py:38
  58.7 1.3 collective-permute-start.7
  61.0 1.1 copy.109
  62.6 2.4 %convolution_multiply_fusion.6 = f32[4,4,64,64]{3,2,1,0:T(8,128)S(1)} fusion(f32[4,4,64]{2,1,0:T(4,128)S(1)} %reduce_window_sum.11, pred[64,64]{1,0:T(8,128)(4,1)S(1)} %iota_compare_fusion.3, f32[4,64,4,128]{3,2,1,0:T(4,128)} %copy-done.10, f32[4,4,64]{2,1,0:T(4,128)S(1)} %copy-done.29, f32[4,64,4,128]{3,2,1,0:T(4,128)} %copy-done.12, ...), kind=kOutput, calls=%fused_computation.45 | convolution fusion | flops 101318656 | bytes 1327104 | tf_op jit(solution)/shard_map/...td,...sd->...ts/dot_general | solution.py:77
  65.1 0.7 convolution_subtract_fusion
  66.3 1.9 fusion.35
  69.1 1.5 fusion.167
  70.6 5.3 %collective-permute-start.6 = (bf16[256,512]{1,0:T(8,128)(2,1)}, bf16[256,512]{1,0:T(8,128)(2,1)}, u32[]{:S(2)}, u32[]{:S(2)}) collective-permute-start(bf16[256,512]{1,0:T(8,128)(2,1)} %param.25), channel_id=1, source_target_pairs={{0,12},{4,16},{8,20},{12,24},{16,28},{1,13},{5,17},{9,21},{13,25},... | collective-permute-start | bytes 786440 | tf_op jit(solution)/shard_map/ppermute | solution.py:38
  76.0 2.3 %fusion.157 = (f32[4,256]{1,0:T(4,128)S(1)}, f32[4,256,256]{1,2,0:T(8,128)}) fusion(bf16[256,4,128]{0,2,1:T(8,128)(2,1)} %bitcast.26, pred[256,256]{0,1:T(8,128)(4,1)S(1)} %get-tuple-element.176, bf16[256,512]{1,0:T(8,128)(2,1)S(1)} %copy-done.3), kind=kOutput, calls=%fused_computation.231 | convolution fusion | flops 67894272 | bytes 1642496 | tf_op jit(solution)/shard_map/thd,shd->hts/dot_general | solution.py:84
  78.3 1.9 collective-permute-start.5
  80.2 1.3 fusion.159
  81.6 18.0 %collective-permute-start.4 = (bf16[256,512]{1,0:T(8,128)(2,1)}, bf16[256,512]{1,0:T(8,128)(2,1)}, u32[]{:S(2)}, u32[]{:S(2)}) collective-permute-start(bf16[256,512]{1,0:T(8,128)(2,1)} %param.25), channel_id=1, source_target_pairs={{0,4},{4,8},{8,12},{12,16},{16,20},{20,24},{24,28},{1,5},{5,9},{9,... | collective-permute-start | bytes 786440 | tf_op jit(solution)/shard_map/ppermute | solution.py:38
  99.5 1.3 fusion.158
  100.9 13.2 %collective-permute-done = bf16[256,512]{0,1:T(8,128)(2,1)} collective-permute-done((bf16[256,512]{0,1:T(8,128)(2,1)}, bf16[256,512]{0,1:T(8,128)(2,1)}, u32[]{:S(2)}, u32[]{:S(2)}) %collective-permute-start) | collective-permute-done | bytes 262176 | tf_op jit(solution)/shard_map/ppermute | solution.py:38
  114.0 1.3 fusion.160
  115.4 1.0 fusion.42
  116.4 1.0 fusion.38
  117.4 1.8 copy.96
  119.2 1.8 copy.94
  121.0 1.8 copy.92
  122.8 18.2 %collective-permute-done.4 = bf16[256,512]{1,0:T(8,128)(2,1)} collective-permute-done((bf16[256,512]{1,0:T(8,128)(2,1)}, bf16[256,512]{1,0:T(8,128)(2,1)}, u32[]{:S(2)}, u32[]{:S(2)}) %collective-permute-start.4) | collective-permute-done | bytes 262176 | tf_op jit(solution)/shard_map/ppermute | solution.py:38
  140.9 1.8 copy.90
  142.7 1.5 fusion.46
  144.3 0.8 fusion.136
  145.0 1.6 fusion.33
  148.8 2.6 %all-gather.7.cloned.1.call-done = bf16[32,128,128]{2,1,0:T(8,128)(2,1)} async-done(((bf16[4,128,128]{2,1,0:T(8,128)(2,1)}), bf16[32,128,128]{2,1,0:T(8,128)(2,1)}) %all-gather.7.cloned.1.call-update) | async-done | bytes 1048592 | tf_op jit(solution)/shard_map/all_gather | solution.py:16
  151.5 5.3 %while.29 = (s32[]{:T(128)}, f32[4,128,128]{2,1,0:T(8,128)S(1)}, s32[]{:T(128)}, bf16[8,4,128,128]{3,2,1,0:T(8,128)(2,1)}, bf16[8,4,128,128]{3,2,1,0:T(8,128)(2,1)}, /*index=5*/s32[]{:T(128)}, s32[]{:T(128)}, s32[]{:T(128)}) while((s32[]{:T(128)}, f32[4,128,128]{2,1,0:T(8,128)S(1)}, s32[]{:T(128)}, bf16[8,4,128,128]{3,2,1,0:T(8,128)(2,1)}, ...), condition=%wide.region_6.7_spmd, body=%wide.region_5.6_spmd.sunk | while | flops 100794368 | bytes 1311871 | solution.py:32
  151.5 1.3 convolution_add_fusion.7
  152.9 1.3 convolution_add_fusion.7
  154.2 1.3 convolution_add_fusion.7
  155.5 1.3 convolution_add_fusion.7
  156.8 1.6 fusion.106
  158.5 2.5 %multiply_reduce_fusion = (f32[4,64,4]{1,0,2:T(4,128)S(1)}, f32[4,64,4,128]{3,1,0,2:T(8,128)S(1)}) fusion(f32[4,4,64,128]{3,2,1,0:T(8,128)S(1)} %fusion.106, f32[4,4,64,128]{3,2,1,0:T(8,128)S(1)} %copy-done.14, f32[4,4,64,128]{3,2,1,0:T(8,128)} %copy-done.15, f32[4,4,128,128]{3,2,1,0:T(8,128)} %get-tuple-element.89), kind=kOutput, calls=%fused_computation.109 | convolution fusion | flops 201849856 | bytes 3149824 | tf_op jit(solution)/shard_map/hntd,hnde->hnte/dot_general | solution.py:152
  161.8 1.9 fusion.97
  163.7 1.7 fusion.14
  165.5 29.9 %reduce-scatter.2.cloned.1.call-done = bf16[64,2048]{1,0:T(8,128)(2,1)} async-done(((bf16[256,2048]{1,0:T(8,128)(2,1)}), bf16[64,2048]{1,0:T(8,128)(2,1)}) %reduce-scatter.2.cloned.1.call-update) | async-done | bytes 262160 | tf_op jit(solution)/shard_map/reduce_scatter | solution.py:212
  (153 shorter events, 15.0 us)
Async XLA Ops:
  6.5 155.3 %copy-start = (bf16[512,2048]{1,0:T(8,128)(2,1)S(1)}, bf16[512,2048]{1,0:T(8,128)(2,1)}, u32[]{:S(2)}) copy-start(bf16[512,2048]{1,0:T(8,128)(2,1)} %param.26) | copy-start | bytes 6291460
  6.5 3.9 %copy-start.34 = (f32[256,4]{0,1:T(4,128)S(1)}, f32[256,4]{0,1:T(4,128)}, u32[]{:S(2)}) copy-start(f32[256,4]{0,1:T(4,128)} %param.19) | copy-start | bytes 12292
  6.5 142.3 %all-gather.5.cloned.1.call-start = ((), (), s32[]{:S(2)}) async-start(), calls=%async_computation.2 | async-start | bytes 1179648 | tf_op jit(solution)/shard_map/all_gather | solution.py:16
  8.6 6.0 %copy-start.10 = (f32[4,64,4,128]{3,2,1,0:T(4,128)}, f32[4,64,4,128]{3,2,1,0:T(4,128)S(1)}, u32[]{:S(2)}) copy-start(f32[4,64,4,128]{3,2,1,0:T(4,128)S(1)} %reshape.510) | copy-start | bytes 1572868
  10.0 4.7 %copy-start.12 = (f32[4,64,4,128]{3,2,1,0:T(4,128)}, f32[4,64,4,128]{3,2,1,0:T(4,128)S(1)}, u32[]{:S(2)}) copy-start(f32[4,64,4,128]{3,2,1,0:T(4,128)S(1)} %reshape.511) | copy-start | bytes 1572868
  13.5 1.9 copy-start.30
  20.0 3.3 %copy-start.31 = (f32[4,4,64]{2,1,0:T(4,128)S(1)}, f32[4,4,64]{2,1,0:T(4,128)}, u32[]{:S(2)}) copy-start(f32[4,4,64]{2,1,0:T(4,128)} %copy-done.30) | copy-start | bytes 12292
  20.0 3.3 %copy-start.33 = (f32[4,4,64]{2,1,0:T(4,128)S(1)}, f32[4,4,64]{2,1,0:T(4,128)}, u32[]{:S(2)}) copy-start(f32[4,4,64]{2,1,0:T(4,128)} %get-tuple-element.172) | copy-start | bytes 12292
  22.6 2.7 %copy-start.8 = (f32[4,64,4,128]{3,2,1,0:T(4,128)S(1)}, f32[4,64,4,128]{3,2,1,0:T(4,128)}, u32[]{:S(2)}) copy-start(f32[4,64,4,128]{3,2,1,0:T(4,128)} %reshape.512) | copy-start | bytes 1572868
  23.2 2.7 %copy-start.13 = (f32[4,64,4,128]{3,2,1,0:T(4,128)S(1)}, f32[4,64,4,128]{3,2,1,0:T(4,128)}, u32[]{:S(2)}) copy-start(f32[4,64,4,128]{3,2,1,0:T(4,128)} %copy-done.12) | copy-start | bytes 1572868
  23.2 2.7 %copy-start.32 = (f32[4,4,64]{2,1,0:T(4,128)S(1)}, f32[4,4,64]{2,1,0:T(4,128)}, u32[]{:S(2)}) copy-start(f32[4,4,64]{2,1,0:T(4,128)} %get-tuple-element.171) | copy-start | bytes 12292
  25.2 3.9 %copy-start.38 = (f32[4,4,64,128]{3,2,1,0:T(8,128)}, f32[4,4,64,128]{3,2,1,0:T(8,128)S(1)}, u32[]{:S(2)}) copy-start(f32[4,4,64,128]{3,2,1,0:T(8,128)S(1)} %fusion.77) | copy-start | bytes 1572868
  25.2 3.9 %copy-start.36 = (f32[4,4]{0,1:T(4,128)S(1)}, f32[4,4]{0,1:T(4,128)}, u32[]{:S(2)}) copy-start(f32[4,4]{0,1:T(4,128)} %exponential_bitcast_fusion) | copy-start | bytes 196
  47.2 14.8 %copy-start.37 = (f32[128]{0:T(128)S(1)}, f32[128]{0:T(128)}, u32[]{:S(2)}) copy-start(f32[128]{0:T(128)} %param.22) | copy-start | bytes 1540
  47.2 15.4 %copy-start.29 = (f32[4,4,64]{2,1,0:T(4,128)S(1)}, f32[4,4,64]{2,1,0:T(4,128)}, u32[]{:S(2)}) copy-start(f32[4,4,64]{2,1,0:T(4,128)} %get-tuple-element.192) | copy-start | bytes 12292
  47.9 103.5 %all-gather.7.cloned.1.call-start = ((), (), s32[]{:S(2)}) async-start(), calls=%async_computation.3 | async-start | bytes 1179648 | tf_op jit(solution)/shard_map/all_gather | solution.py:16
  49.8 20.9 %collective-permute-start.3 = (bf16[256,512]{0,1:T(8,128)(2,1)}, bf16[256,512]{0,1:T(8,128)(2,1)}, u32[]{:S(2)}, u32[]{:S(2)}) collective-permute-start(bf16[256,512]{0,1:T(8,128)(2,1)} %copy.76), channel_id=1, source_target_pairs={{0,16},{4,20},{8,24},{12,28},{1,17},{5,21},{9,25},{13,29},{2,18},{... | collective-permute-start | bytes 786440 | tf_op jit(solution)/shard_map/ppermute | solution.py:38
  51.1 27.2 %collective-permute-start.1 = (bf16[256,512]{0,1:T(8,128)(2,1)}, bf16[256,512]{0,1:T(8,128)(2,1)S(1)}, u32[]{:S(2)}, u32[]{:S(2)}) collective-permute-start(bf16[256,512]{0,1:T(8,128)(2,1)} %copy.76), channel_id=1, source_target_pairs={{0,8},{4,12},{8,16},{12,20},{16,24},{20,28},{1,9},{5,13},{9,17},{1... | collective-permute-start | bytes 786440 | tf_op jit(solution)/shard_map/ppermute | solution.py:38
  54.3 27.3 %collective-permute-start.2 = (bf16[256,512]{0,1:T(8,128)(2,1)}, bf16[256,512]{0,1:T(8,128)(2,1)}, u32[]{:S(2)}, u32[]{:S(2)}) collective-permute-start(bf16[256,512]{0,1:T(8,128)(2,1)} %copy.76), channel_id=1, source_target_pairs={{0,12},{4,16},{8,20},{12,24},{16,28},{1,13},{5,17},{9,21},{13,25},... | collective-permute-start | bytes 786440 | tf_op jit(solution)/shard_map/ppermute | solution.py:38
  56.5 57.5 %collective-permute-start = (bf16[256,512]{0,1:T(8,128)(2,1)}, bf16[256,512]{0,1:T(8,128)(2,1)}, u32[]{:S(2)}, u32[]{:S(2)}) collective-permute-start(bf16[256,512]{0,1:T(8,128)(2,1)} %copy.76), channel_id=1, source_target_pairs={{0,4},{4,8},{8,12},{12,16},{16,20},{20,24},{24,28},{1,5},{5,9},{9,... | collective-permute-start | bytes 786440 | tf_op jit(solution)/shard_map/ppermute | solution.py:38
  58.7 58.6 %collective-permute-start.7 = (bf16[256,512]{1,0:T(8,128)(2,1)}, bf16[256,512]{1,0:T(8,128)(2,1)}, u32[]{:S(2)}, u32[]{:S(2)}) collective-permute-start(bf16[256,512]{1,0:T(8,128)(2,1)} %param.25), channel_id=1, source_target_pairs={{0,16},{4,20},{8,24},{12,28},{1,17},{5,21},{9,25},{13,29},{2,18},{... | collective-permute-start | bytes 786440 | tf_op jit(solution)/shard_map/ppermute | solution.py:38
  60.7 134.7 %reduce-scatter.2.cloned.1.call-start = ((), (), s32[]{:S(2)}) async-start(), calls=%async_computation.1 | async-start | bytes 1310720 | tf_op jit(solution)/shard_map/reduce_scatter | solution.py:212
  62.6 2.5 %copy-start.11 = (f32[4,64,4,128]{3,2,1,0:T(4,128)S(1)}, f32[4,64,4,128]{3,2,1,0:T(4,128)}, u32[]{:S(2)}) copy-start(f32[4,64,4,128]{3,2,1,0:T(4,128)} %copy-done.10) | copy-start | bytes 1572868
  62.6 2.5 %copy-start.39 = (f32[4,4,64,128]{3,2,1,0:T(8,128)S(1)}, f32[4,4,64,128]{3,2,1,0:T(8,128)}, u32[]{:S(2)}) copy-start(f32[4,4,64,128]{3,2,1,0:T(8,128)} %copy-done.38) | copy-start | bytes 1572868
  65.0 1.2 copy-start.16
  65.1 3.7 %copy-start.3 = (bf16[256,512]{1,0:T(8,128)(2,1)S(1)}, bf16[256,512]{1,0:T(8,128)(2,1)}, u32[]{:S(2)}) copy-start(bf16[256,512]{1,0:T(8,128)(2,1)} %param.23) | copy-start | bytes 786436
  65.1 3.7 %copy-start.25 = (bf16[256,512]{1,0:T(8,128)(2,1)S(1)}, bf16[256,512]{1,0:T(8,128)(2,1)}, u32[]{:S(2)}) copy-start(bf16[256,512]{1,0:T(8,128)(2,1)} %param.24) | copy-start | bytes 786436
  65.8 3.3 %copy-start.15 = (f32[4,4,64,128]{3,2,1,0:T(8,128)}, f32[4,4,64,128]{3,2,1,0:T(8,128)S(1)}, u32[]{:S(2)}) copy-start(f32[4,4,64,128]{3,2,1,0:T(8,128)S(1)} %convolution_subtract_fusion) | copy-start | bytes 1572868
  68.7 9.5 %copy-start.19 = (pred[256,256]{0,1:T(8,128)(4,1)}, pred[256,256]{0,1:T(8,128)(4,1)S(1)}, u32[]{:S(2)}) copy-start(pred[256,256]{0,1:T(8,128)(4,1)S(1)} %get-tuple-element.176) | copy-start | bytes 196612
  68.7 47.6 %copy-start.20 = (pred[256,256]{0,1:T(8,128)(4,1)}, pred[256,256]{0,1:T(8,128)(4,1)S(1)}, u32[]{:S(2)}) copy-start(pred[256,256]{0,1:T(8,128)(4,1)S(1)} %get-tuple-element.178) | copy-start | bytes 196612
  68.7 47.6 %copy-start.22 = (pred[256,256]{0,1:T(8,128)(4,1)}, pred[256,256]{0,1:T(8,128)(4,1)S(1)}, u32[]{:S(2)}) copy-start(pred[256,256]{0,1:T(8,128)(4,1)S(1)} %get-tuple-element.174) | copy-start | bytes 196612
  69.1 47.3 %copy-start.4 = (f32[4,256,256]{1,2,0:T(8,128)}, f32[4,256,256]{1,2,0:T(8,128)S(1)}, u32[]{:S(2)}) copy-start(f32[4,256,256]{1,2,0:T(8,128)S(1)} %get-tuple-element.190) | copy-start | bytes 3145732
  70.6 48.5 %collective-permute-start.6 = (bf16[256,512]{1,0:T(8,128)(2,1)}, bf16[256,512]{1,0:T(8,128)(2,1)}, u32[]{:S(2)}, u32[]{:S(2)}) collective-permute-start(bf16[256,512]{1,0:T(8,128)(2,1)} %param.25), channel_id=1, source_target_pairs={{0,12},{4,16},{8,20},{12,24},{16,28},{1,13},{5,17},{9,21},{13,25},... | collective-permute-start | bytes 786440 | tf_op jit(solution)/shard_map/ppermute | solution.py:38
  78.3 1.9 copy-start.24
  78.3 42.7 %collective-permute-start.5 = (bf16[256,512]{1,0:T(8,128)(2,1)}, bf16[256,512]{1,0:T(8,128)(2,1)}, u32[]{:S(2)}, u32[]{:S(2)}) collective-permute-start(bf16[256,512]{1,0:T(8,128)(2,1)} %param.25), channel_id=1, source_target_pairs={{0,8},{4,12},{8,16},{12,20},{16,24},{20,28},{1,9},{5,13},{9,17},{1... | collective-permute-start | bytes 786440 | tf_op jit(solution)/shard_map/ppermute | solution.py:38
  81.6 59.4 %collective-permute-start.4 = (bf16[256,512]{1,0:T(8,128)(2,1)}, bf16[256,512]{1,0:T(8,128)(2,1)}, u32[]{:S(2)}, u32[]{:S(2)}) collective-permute-start(bf16[256,512]{1,0:T(8,128)(2,1)} %param.25), channel_id=1, source_target_pairs={{0,4},{4,8},{8,12},{12,16},{16,20},{20,24},{24,28},{1,5},{5,9},{9,... | collective-permute-start | bytes 786440 | tf_op jit(solution)/shard_map/ppermute | solution.py:38
  100.9 16.5 %copy-start.1 = (f32[4,256,256]{1,2,0:T(8,128)}, f32[4,256,256]{1,2,0:T(8,128)S(1)}, u32[]{:S(2)}) copy-start(f32[4,256,256]{1,2,0:T(8,128)S(1)} %get-tuple-element.184) | copy-start | bytes 3145732
  115.4 2.0 copy-start.6
  115.4 2.0 copy-start.27
  142.7 4.0 %copy-start.2 = (f32[4,256,256]{1,2,0:T(8,128)S(1)}, f32[4,256,256]{1,2,0:T(8,128)}, u32[]{:S(2)}) copy-start(f32[4,256,256]{1,2,0:T(8,128)} %copy-done.1) | copy-start | bytes 3145732
  142.7 4.0 %copy-start.18 = (bf16[256,512]{0,1:T(8,128)(2,1)S(1)}, bf16[256,512]{0,1:T(8,128)(2,1)}, u32[]{:S(2)}) copy-start(bf16[256,512]{0,1:T(8,128)(2,1)} %copy.94) | copy-start | bytes 786436
  144.3 2.8 %copy-start.17 = (bf16[256,512]{0,1:T(8,128)(2,1)S(1)}, bf16[256,512]{0,1:T(8,128)(2,1)}, u32[]{:S(2)}) copy-start(bf16[256,512]{0,1:T(8,128)(2,1)} %copy.92) | copy-start | bytes 786436
  146.7 1.3 copy-start.5
  146.7 1.3 copy-start.23
  147.1 1.3 copy-start.7
  147.1 1.3 copy-start.21
  147.1 1.4 copy-start.26
  147.1 1.3 copy-start.28
  151.5 7.0 %copy-start.14 = (f32[4,4,64,128]{3,2,1,0:T(8,128)S(1)}, f32[4,4,64,128]{3,2,1,0:T(8,128)}, u32[]{:S(2)}) copy-start(f32[4,4,64,128]{3,2,1,0:T(8,128)} %fusion.167) | copy-start | bytes 1572868
  158.4 3.4 %copy-start.35 = (f32[512]{0:T(512)S(1)}, f32[512]{0:T(512)}, u32[]{:S(2)}) copy-start(f32[512]{0:T(512)} %broadcast_bitcast_fusion) | copy-start | bytes 6148
  161.8 1.9 copy-start.9
Sparse Core Ops, SparseCore 0:
  48.1 47.3 all-gather.4
  97.6 53.8 all-gather.6
  165.6 29.7 reduce-scatter.1
where the time goes:
time: 205 us; the launch traced here: 202 us
  waiting for transfers between devices  64 us (31%)
  matrix products  56.8 us (28%)
  starting transfers between devices  35.5 us (17%)
  local copies, waits for them, and re-layouts  18.9 us (9%)
  between operations  14.1 us (7%)
  other arithmetic  12.3 us (6%)
    ppermute x8, starting transfers between devices, passed_along(): return lax.ppermute(block, axis, route)  35.4 us
    ppermute x8, waiting for transfers between devices, passed_along(): return lax.ppermute(block, axis, route)  31.3 us
    reduce_scatter x1, waiting for transfers between devices, shards(): lax.psum_scatter(running_partial_sum.astype(jnp.bfloat16), 'head', scatte...  29.9 us
    dot_general x8, matrix products, chain_pairs(): jnp.einsum('hij,hjk->hik', later[0], earlier[1], precision=highest)  10.8 us
    ppermute x4, local copies, waits for them, and re-layouts, passed_along(): return lax.ppermute(block, axis, route)  7.17 us
    dot_general x5, matrix products, window_block(): jnp.einsum('thd,shd->hts', queries, keys_in, preferred_element_type=jnp.f...  6.57 us
    dot_general x4, matrix products, chain_pairs(): matrix = jnp.einsum('hij,hjk->hik', later[0], earlier[0], precision=highest)  5.35 us
    transpose x3, local copies, waits for them, and re-layouts, heads_blocks(): return array.astype(jnp.float32).reshape(blocks, block_len, local_heads,...  4.34 us
  transfers between devices with their start and end apart: 11, of which 4 were waited for; matrix products, arithmetic and copies ran while one was open for 16% of the time, Pallas kernels for 0%

commit v1 on v0

v1 whole, which is shorter than its diff:
```python
import functools

import jax
import jax.numpy as jnp
from jax import lax
from jax.experimental import pallas as pl
from jax.experimental.pallas import tpu as pltpu
from jax.sharding import PartitionSpec as P

DH = 128
WINDOW = 1024
F32 = jnp.float32
BF16 = jnp.bfloat16


def mm(a, b, dims=((1,), (0,))):
    return lax.dot_general(
        a.astype(BF16), b.astype(BF16), (dims, ((), ())), preferred_element_type=F32
    )


def unit_rows(array):
    return array * lax.rsqrt(jnp.sum(array * array, axis=-1, keepdims=True) + 1e-06)


def grids(rows):
    i = lax.broadcasted_iota(jnp.int32, (rows, rows), 0)
    j = lax.broadcasted_iota(jnp.int32, (rows, rows), 1)
    return i, j


def unit_inverses(lowers):
    rows = lowers[0].shape[0]
    i, j = grids(rows)
    apart = i ^ j
    lower = i > j
    first = jnp.where(i == j, 1.0, 0.0)
    inverses = [first - jnp.where(lower & (apart == 1), a, 0.0) for a in lowers]
    level = 1
    while (1 << level) < rows:
        band = lower & ((apart >> level) == 1)
        rounded = [x.astype(BF16) for x in inverses]
        left = [mm(x, jnp.where(band, a, 0.0)) for x, a in zip(rounded, lowers)]
        inverses = [x - mm(y, r) for x, y, r in zip(inverses, left, rounded)]
        level += 1
    return inverses


def delta_local(queries, keys, values, betas, columns, lines):
    heads = range(len(queries))
    rows = queries[0].shape[0]
    i, j = grids(rows)
    ks = [unit_rows(k.astype(F32)) for k in keys]
    qs = [unit_rows(q.astype(F32)) * DH ** (-0.5) for q in queries]
    kb = [k.astype(BF16) for k in ks]
    ratio = [
        jnp.where(i >= j, jnp.exp(jnp.where(i >= j, columns[h] - lines[h], 0.0)), 0.0) for h in heads
    ]
    lowers = [
        jnp.where(i > j, betas[h] * ratio[h] * mm(kb[h], kb[h], ((1,), (1,))), 0.0) for h in heads
    ]
    mixing = [(ratio[h] * mm(qs[h], kb[h], ((1,), (1,)))).astype(BF16) for h in heads]
    inverses = unit_inverses(lowers)
    decayed = [jnp.exp(columns[h]) for h in heads]
    right = [
        jnp.concatenate(
            [values[h].astype(F32) * betas[h], ks[h] * (betas[h] * decayed[h])], axis=1
        )
        for h in heads
    ]
    solved = [mm(inverses[h], right[h]).astype(BF16) for h in heads]
    last = [columns[h][rows - 1 :, :] for h in heads]
    ends = [ks[h] * jnp.exp(last[h] - columns[h]) for h in heads]
    written = [mm(ends[h], solved[h], ((0,), (0,))) for h in heads]
    read = [mm(mixing[h], solved[h]) for h in heads]
    a, b = lax.broadcasted_iota(jnp.int32, (DH, DH), 0), lax.broadcasted_iota(jnp.int32, (DH, DH), 1)
    moves = [
        jnp.where(a == b, jnp.exp(last[h]), 0.0) - written[h][:, DH:] for h in heads
    ]
    adds = [written[h][:, :DH] for h in heads]
    own = [read[h][:, :DH] for h in heads]
    carry = [decayed[h] * qs[h] - read[h][:, DH:] for h in heads]
    return moves, adds, own, carry


def kernel(
    n,
    heads,
    dq, dk, dv, gb, gate, gain, aq, ak, av, wd_any, wa_any,
    out,
    kv, own_out, carry, pair_own, pair_in, joined, s_in, s_out,
    top, den, num, dh, ah, wd, wa, part_out, part_in, kept, sum_out, sum_in,
    w_sem, kv_send, kv_recv, pair_sem, s_sem, part_sem, sum_sem,
):
    c = lax.axis_index("ctx")
    h = lax.axis_index("head")
    odd = lax.rem(c, 2)
    even = 1 - odd
    partner = c + 1 - 2 * odd
    above, below = c + 2, c - 2
    has_up, has_down = above < n, c >= 2
    sibling = h + 1 - 2 * lax.rem(h, 2)
    across = lax.rem(h + 2, 4)
    diagonal = lax.rem(sibling + 2, 4)
    rows = dq.shape[0]

    loads = [
        pltpu.make_async_copy(wd_any, wd, w_sem.at[0]),
        pltpu.make_async_copy(wa_any, wa, w_sem.at[1]),
    ]
    for load in loads:
        load.start()

    barrier = pltpu.get_barrier_semaphore()
    for target in ({"ctx": partner}, {"head": sibling}, {"head": across}):
        pl.semaphore_signal(barrier, inc=1, device_id=target, device_id_type=pl.DeviceIdType.MESH)

    @pl.when(has_up)
    def _():
        pl.semaphore_signal(barrier, inc=1, device_id={"ctx": above}, device_id_type=pl.DeviceIdType.MESH)

    @pl.when(has_down)
    def _():
        pl.semaphore_signal(barrier, inc=1, device_id={"ctx": below}, device_id_type=pl.DeviceIdType.MESH)

    pl.semaphore_wait(barrier, 3 + has_up.astype(jnp.int32) + has_down.astype(jnp.int32))

    def remote(src, dst, send, recv, target):
        return pltpu.make_async_remote_copy(
            src_ref=src, dst_ref=dst, send_sem=send, recv_sem=recv,
            device_id=target, device_id_type=pl.DeviceIdType.MESH,
        )

    def kv_copy(route, part, src, back, target):
        return remote(
            src, kv.at[back - 1, part], kv_send.at[route, part], kv_recv.at[back - 1, part], {"ctx": target}
        )

    mine = (ak, av)

    def routes(part):
        return [
            (has_up, lambda: kv_copy(0, part, mine[part], 2, above)),
            (even == 1, lambda: kv_copy(1, part, mine[part], 1, partner)),
            (has_down & has_up, lambda: kv_copy(2, part, kv.at[1, part], 4, above)),
            (has_down & (even == 1), lambda: kv_copy(3, part, kv.at[1, part], 3, partner)),
            (has_down & (odd == 1), lambda: kv_copy(3, part, kv.at[1, part], 1, partner)),
            ((c >= 4) & (odd == 1), lambda: kv_copy(4, part, kv.at[3, part], 3, partner)),
        ]

    def start(which):
        for part in (0, 1):
            for item in which:
                condition, copy = routes(part)[item]

                @pl.when(condition)
                def _():
                    copy().start()

    def arrived(back, part):
        kv_copy(0, part, mine[part], back, above).wait_recv()

    start((0, 1))

    i, j = grids(rows)
    summed = lax.dot_general(
        jnp.where(i >= j, 1.0, 0.0), gb[...], (((1,), (0,)), ((), ())),
        precision=lax.Precision.HIGHEST, preferred_element_type=F32,
    )
    turned = summed.T

    def cut(ref, head):
        return ref[:, head * DH : (head + 1) * DH]

    for some in ([0, 1], [2, 3]):
        moves, adds, own, carries = delta_local(
            [cut(dq, x) for x in some],
            [cut(dk, x) for x in some],
            [cut(dv, x) for x in some],
            [gb[:, x : x + 1] for x in some],
            [summed[:, heads + x : heads + x + 1] for x in some],
            [turned[heads + x : heads + x + 1, :] for x in some],
        )
        for at, x in enumerate(some):
            pair_own[x, :, :DH] = moves[at].astype(BF16)
            pair_own[x, :, DH:] = adds[at].astype(BF16)
            own_out[x] = own[at]
            carry[x] = carries[at].astype(BF16)

    pair_copy = remote(pair_own, pair_in, pair_sem.at[0], pair_sem.at[1], {"ctx": partner})
    pair_copy.start()

    @pl.when(has_down)
    def _():
        for part in (0, 1):
            arrived(2, part)

    start((2, 3, 4))

    def attend(back):
        keys, vals = mine if back == 0 else (kv.at[back - 1, 0], kv.at[back - 1, 1])
        for x in range(heads):
            scores = mm(cut(aq, x), keys[:, x * DH : (x + 1) * DH], ((1,), (1,))) * DH ** (-0.5)
            if back == 0:
                scores = jnp.where(i >= j, scores, -1e30)
            if back == WINDOW // rows:
                scores = jnp.where(j > i, scores, -1e30)
            block_top = jnp.max(scores, axis=-1, keepdims=True)
            if back == 0:
                high = block_top
            else:
                before = top[x][:, :1]
                high = jnp.maximum(before, block_top)
            weights = jnp.exp(scores - high)
            block_den = jnp.sum(weights, axis=-1, keepdims=True)
            block_num = mm(weights, vals[:, x * DH : (x + 1) * DH])
            if back > 0:
                factor = jnp.exp(before - high)
                block_den = block_den + factor * den[x][:, :1]
                block_num = block_num + factor * num[x]
            top[x] = jnp.broadcast_to(high, (rows, DH))
            den[x] = jnp.broadcast_to(block_den, (rows, DH))
            num[x] = block_num

    attend(0)

    pair_copy.wait_recv()
    for x in range(heads):
        mine_pair, its_pair = pair_own[x].astype(F32), pair_in[x].astype(F32)
        first = jnp.where(even == 1, mine_pair, its_pair)
        second = jnp.where(even == 1, its_pair, mine_pair)
        both = mm(second[:, :DH], first)
        joined[x, :, :DH] = both[:, :DH]
        joined[x, :, DH:] = both[:, DH:] + second[:, DH:]

    state_copy = remote(s_out, s_in, s_sem.at[0], s_sem.at[1], {"ctx": above})

    @pl.when(c < 2)
    def _():
        s_in[...] = jnp.zeros_like(s_in)

    @pl.when(has_up)
    def _():
        @pl.when(has_down)
        def _():
            state_copy.wait_recv()

        for x in range(heads):
            s_out[x] = (mm(joined[x, :, :DH], s_in[x]) + joined[x, :, DH:]).astype(BF16)
        state_copy.start()

    @pl.when(has_down)
    def _():
        attend(2)

    @pl.when(c >= 1)
    def _():
        for part in (0, 1):
            arrived(1, part)
        attend(1)

    @pl.when(c >= 4)
    def _():
        for part in (0, 1):
            arrived(4, part)

    start((5,))

    @pl.when(c >= 4)
    def _():
        attend(4)

    @pl.when(c >= 3)
    def _():
        for part in (0, 1):
            arrived(3, part)
        attend(3)

    for x in range(heads):
        ah[:, x * DH : (x + 1) * DH] = (num[x] / den[x]).astype(BF16)

    @pl.when(has_down & (above >= n))
    def _():
        state_copy.wait_recv()

    for x in range(heads):
        state = s_in[x].astype(F32)
        its_pair = pair_in[x].astype(F32)
        moved = mm(its_pair[:, :DH], state) + its_pair[:, DH:]
        state = jnp.where(odd == 1, moved, state)
        raw = own_out[x] + mm(carry[x], state)
        gates = cut(gate, x).astype(F32)
        scale = lax.rsqrt(jnp.mean(raw * raw, axis=-1, keepdims=True) + 1e-06)
        normed = raw * scale * gain[...] * (gates / (1.0 + jnp.exp(-gates)))
        dh[:, x * DH : (x + 1) * DH] = normed.astype(BF16)

    for load in loads:
        load.wait()
    quarter = rows // 4
    width = out.shape[1]
    tile = 512

    def project(targets, store):
        ds = [pl.ds(pl.multiple_of(t * quarter, quarter), quarter) for t in targets]
        d_rows = jnp.concatenate([dh[d, :] for d in ds], axis=0)
        a_rows = jnp.concatenate([ah[d, :] for d in ds], axis=0)
        for low in range(0, width, tile):
            part = mm(d_rows, wd[:, low : low + tile]) + mm(a_rows, wa[:, low : low + tile])
            for at in range(2):
                store[at, :, low : low + tile] = part[at * quarter : (at + 1) * quarter].astype(BF16)

    project((sibling, diagonal), part_out)
    part_copy = remote(part_out, part_in, part_sem.at[0], part_sem.at[1], {"head": sibling})
    part_copy.start()
    project((h, across), kept)
    part_copy.wait_recv()
    sum_out[...] = (kept[1].astype(F32) + part_in[1].astype(F32)).astype(BF16)
    sum_copy = remote(sum_out, sum_in, sum_sem.at[0], sum_sem.at[1], {"head": across})
    sum_copy.start()
    kept_sum = kept[0].astype(F32) + part_in[0].astype(F32)
    sum_copy.wait_recv()
    out[...] = (kept_sum + sum_in[...].astype(F32)).astype(BF16)

    part_copy.wait_send()
    sum_copy.wait_send()
    pair_copy.wait_send()

    @pl.when(has_up)
    def _():
        state_copy.wait_send()

    for part in (0, 1):
        for condition, copy in routes(part):

            @pl.when(condition)
            def _():
                copy().wait_send()


def shards(
    n,
    delta_q, delta_k, delta_v, beta, log_decay, out_gate, norm_gain,
    attn_q, attn_k, attn_v, w_delta_out, w_attn_out,
):
    rows, columns = delta_q.shape
    heads = columns // DH
    width = w_delta_out.shape[1]
    gb = jnp.concatenate(
        [beta, log_decay, jnp.zeros((rows, DH - 2 * heads), F32)], axis=1
    )
    vmem = pl.BlockSpec(memory_space=pltpu.VMEM)
    hbm = pl.BlockSpec(memory_space=pl.ANY)
    quarter = rows // 4
    return pl.pallas_call(
        functools.partial(kernel, n, heads),
        out_shape=jax.ShapeDtypeStruct((quarter, width), BF16),
        in_specs=[vmem] * 9 + [hbm] * 2,
        out_specs=vmem,
        scratch_shapes=[
            pltpu.VMEM((4, 2, rows, columns), BF16),
            pltpu.VMEM((heads, rows, DH), F32),
            pltpu.VMEM((heads, rows, DH), BF16),
            pltpu.VMEM((heads, DH, 2 * DH), BF16),
            pltpu.VMEM((heads, DH, 2 * DH), BF16),
            pltpu.VMEM((heads, DH, 2 * DH), F32),
            pltpu.VMEM((heads, DH, DH), BF16),
            pltpu.VMEM((heads, DH, DH), BF16),
            pltpu.VMEM((heads, rows, DH), F32),
            pltpu.VMEM((heads, rows, DH), F32),
            pltpu.VMEM((heads, rows, DH), F32),
            pltpu.VMEM((rows, columns), BF16),
            pltpu.VMEM((rows, columns), BF16),
            pltpu.VMEM(w_delta_out.shape, BF16),
            pltpu.VMEM(w_attn_out.shape, BF16),
            pltpu.VMEM((2, quarter, width), BF16),
            pltpu.VMEM((2, quarter, width), BF16),
            pltpu.VMEM((2, quarter, width), BF16),
            pltpu.VMEM((quarter, width), BF16),
            pltpu.VMEM((quarter, width), BF16),
            pltpu.SemaphoreType.DMA((2,)),
            pltpu.SemaphoreType.DMA((5, 2)),
            pltpu.SemaphoreType.DMA((4, 2)),
            pltpu.SemaphoreType.DMA((2,)),
            pltpu.SemaphoreType.DMA((2,)),
            pltpu.SemaphoreType.DMA((2,)),
            pltpu.SemaphoreType.DMA((2,)),
        ],
        compiler_params=pltpu.CompilerParams(
            collective_id=0, has_side_effects=True, vmem_limit_bytes=48 * 1024 * 1024
        ),
        cost_estimate=pl.CostEstimate(flops=4_000_000_000, bytes_accessed=8_000_000, transcendentals=2_000_000),
    )(
        delta_q, delta_k, delta_v, gb, out_gate, norm_gain.reshape(1, DH),
        attn_q, attn_k, attn_v, w_delta_out, w_attn_out,
    )


def solution(mesh):
    return jax.shard_map(
        functools.partial(shards, mesh.shape["ctx"]),
        mesh=mesh,
        in_specs=(
            P("ctx", "head"),
            P("ctx", "head"),
            P("ctx", "head"),
            P("ctx", "head"),
            P("ctx", "head"),
            P("ctx", "head"),
            P(),
            P("ctx", "head"),
            P("ctx", "head"),
            P("ctx", "head"),
            P("head", None),
            P("head", None),
        ),
        out_specs=P(("ctx", "head"), None),
        check_vma=False,
    )
```

time: 205 us -> 71.6 us (0.35); the launches traced: 202 us -> 71.1 us
  waiting for transfers between devices: 64 us -> 0 us
  Pallas kernels: 0 us -> 59.7 us
  matrix products: 56.8 us -> 0 us
  starting transfers between devices: 35.5 us -> 0 us
  between operations: 14.1 us -> 0.05 us
  other arithmetic: 12.3 us -> 0.1 us
  local copies, waits for them, and re-layouts: 18.9 us -> 11.3 us
    pallas_call x0 -> x1, Pallas kernels: none -> 59.7 us  [shards(): pl.pallas_call(functools.partial(kernel, n, heads), out_shape=jax.ShapeDt...]
    dot_general x45 -> x0, matrix products: 56.8 us -> none  [the longest x8 10.8 us: chain_pairs(): jnp.einsum('hij,hjk->hik', later[0], earlier[1], precision=highest)]
    ppermute x8 -> x0, starting transfers between devices: 35.4 us -> none  [passed_along(): return lax.ppermute(block, axis, route)]
    ppermute x8 -> x0, waiting for transfers between devices: 31.3 us -> none  [passed_along(): return lax.ppermute(block, axis, route)]
    reduce_scatter x1 -> x0, waiting for transfers between devices: 29.9 us -> none  [shards(): lax.psum_scatter(running_partial_sum.astype(jnp.bfloat16), 'head', scatte...]
    unnamed x81 -> x21, local copies, waits for them, and re-layouts: 3.01 us -> 11.2 us
    ppermute x4 -> x0, local copies, waits for them, and re-layouts: 7.17 us -> none  [passed_along(): return lax.ppermute(block, axis, route)]
    transpose x3 -> x0, local copies, waits for them, and re-layouts: 4.34 us -> none  [heads_blocks(): return array.astype(jnp.float32).reshape(blocks, block_len, local_heads,...]
  transfers between devices with their start and end apart: 11 -> 0, of which waited for: 4 -> 0; matrix products, arithmetic and copies ran while one was open for 16% -> 0% of each run, Pallas kernels for 0% -> 0%
where the time goes in v1:
time: 71.6 us; the launch traced here: 71.1 us
  Pallas kernels  59.7 us (83%)
  local copies, waits for them, and re-layouts  11.3 us (16%)
    pallas_call x1, Pallas kernels, shards(): pl.pallas_call(functools.partial(kernel, n, heads), out_shape=jax.ShapeDt...  59.7 us
    unnamed x21, local copies, waits for them, and re-layouts  11.2 us

profile of v1, /device:TPU:17, one launch (start us, length us, event | category | flops | bytes accessed | tf_op | source)
XLA Modules:
  0.0 71.1 jit_solution(14932825468019533000)
XLA Ops:
  0.0 0.1 pad.2.clone
  0.1 0.8 %copy.13 = f32[256,4]{1,0:T(8,128)S(1)} copy(f32[256,4]{0,1:T(4,128)} %param.15) | data formatting | bytes 8192 | tf_op args[3]
  0.9 0.8 %copy.14 = f32[256,4]{1,0:T(8,128)S(1)} copy(f32[256,4]{0,1:T(4,128)} %param.16) | data formatting | bytes 8192 | tf_op args[4]
  1.7 0.1 maximum_maximum_fusion.gb
  1.8 0.0 copy-start
  1.9 1.6 %copy-done = bf16[512,2048]{1,0:T(8,128)(2,1)S(1)} copy-done((bf16[512,2048]{1,0:T(8,128)(2,1)S(1)}, bf16[512,2048]{1,0:T(8,128)(2,1)}, u32[]{:S(2)}) %copy-start) | copy-done | bytes 2097176
  3.4 0.0 copy-start.1
  3.4 0.9 %copy-done.1 = bf16[256,512]{1,0:T(8,128)(2,1)S(1)} copy-done((bf16[256,512]{1,0:T(8,128)(2,1)S(1)}, bf16[256,512]{1,0:T(8,128)(2,1)}, u32[]{:S(2)}) %copy-start.1) | copy-done | bytes 262168
  4.4 0.0 copy-start.2
  4.4 0.9 %copy-done.2 = bf16[256,512]{1,0:T(8,128)(2,1)S(1)} copy-done((bf16[256,512]{1,0:T(8,128)(2,1)S(1)}, bf16[256,512]{1,0:T(8,128)(2,1)}, u32[]{:S(2)}) %copy-start.2) | copy-done | bytes 262168
  5.3 0.0 copy-start.3
  5.3 0.9 %copy-done.3 = bf16[256,512]{1,0:T(8,128)(2,1)S(1)} copy-done((bf16[256,512]{1,0:T(8,128)(2,1)S(1)}, bf16[256,512]{1,0:T(8,128)(2,1)}, u32[]{:S(2)}) %copy-start.3) | copy-done | bytes 262168
  6.3 0.0 copy-start.4
  6.3 0.9 %copy-done.4 = bf16[256,512]{1,0:T(8,128)(2,1)S(1)} copy-done((bf16[256,512]{1,0:T(8,128)(2,1)S(1)}, bf16[256,512]{1,0:T(8,128)(2,1)}, u32[]{:S(2)}) %copy-start.4) | copy-done | bytes 262168
  7.2 0.0 copy-start.5
  7.2 0.9 %copy-done.5 = bf16[256,512]{1,0:T(8,128)(2,1)S(1)} copy-done((bf16[256,512]{1,0:T(8,128)(2,1)S(1)}, bf16[256,512]{1,0:T(8,128)(2,1)}, u32[]{:S(2)}) %copy-start.5) | copy-done | bytes 262168
  8.2 0.0 copy-start.6
  8.2 0.9 %copy-done.6 = bf16[256,512]{1,0:T(8,128)(2,1)S(1)} copy-done((bf16[256,512]{1,0:T(8,128)(2,1)S(1)}, bf16[256,512]{1,0:T(8,128)(2,1)}, u32[]{:S(2)}) %copy-start.6) | copy-done | bytes 262168
  9.1 0.0 copy-start.7
  9.1 0.9 %copy-done.7 = bf16[256,512]{1,0:T(8,128)(2,1)S(1)} copy-done((bf16[256,512]{1,0:T(8,128)(2,1)S(1)}, bf16[256,512]{1,0:T(8,128)(2,1)}, u32[]{:S(2)}) %copy-start.7) | copy-done | bytes 262168
  10.1 0.0 copy-start.8
  10.1 0.7 copy-done.8
  10.7 59.7 %shard_map.118 = bf16[64,2048]{1,0:T(8,128)(2,1)S(1)} custom-call(bf16[256,512]{1,0:T(8,128)(2,1)S(1)} %copy-done.1, bf16[256,512]{1,0:T(8,128)(2,1)S(1)} %copy-done.2, bf16[256,512]{1,0:T(8,128)(2,1)S(1)} %copy-done.3, f32[256,128]{1,0:T(8,128)S(1)} %maximum_maximum_fusion.gb, bf16[256,512]{1,0:T(8,128)(2,1)S(1)} %copy-done.4, f32[1,128]{1,0:T(1,128)S(1)} %bitcast.1, ...), custom_call_target="tpu_custom_call" | custom-call | flops 4000000000 | bytes 8000000 | tf_op jit(solution)/shard_map/pallas_call | solution.py:354
  70.4 0.7 copy.16
  (1 shorter events, 0.0 us)
Async XLA Ops:
  1.8 1.6 %copy-start = (bf16[512,2048]{1,0:T(8,128)(2,1)S(1)}, bf16[512,2048]{1,0:T(8,128)(2,1)}, u32[]{:S(2)}) copy-start(bf16[512,2048]{1,0:T(8,128)(2,1)} %wd_any.1) | copy-start | bytes 6291460
  3.4 0.9 %copy-start.1 = (bf16[256,512]{1,0:T(8,128)(2,1)S(1)}, bf16[256,512]{1,0:T(8,128)(2,1)}, u32[]{:S(2)}) copy-start(bf16[256,512]{1,0:T(8,128)(2,1)} %dq.1) | copy-start | bytes 786436
  4.4 0.9 %copy-start.2 = (bf16[256,512]{1,0:T(8,128)(2,1)S(1)}, bf16[256,512]{1,0:T(8,128)(2,1)}, u32[]{:S(2)}) copy-start(bf16[256,512]{1,0:T(8,128)(2,1)} %dk.1) | copy-start | bytes 786436
  5.3 0.9 %copy-start.3 = (bf16[256,512]{1,0:T(8,128)(2,1)S(1)}, bf16[256,512]{1,0:T(8,128)(2,1)}, u32[]{:S(2)}) copy-start(bf16[256,512]{1,0:T(8,128)(2,1)} %dv.1) | copy-start | bytes 786436
  6.3 0.9 %copy-start.4 = (bf16[256,512]{1,0:T(8,128)(2,1)S(1)}, bf16[256,512]{1,0:T(8,128)(2,1)}, u32[]{:S(2)}) copy-start(bf16[256,512]{1,0:T(8,128)(2,1)} %gate.1) | copy-start | bytes 786436
  7.2 0.9 %copy-start.5 = (bf16[256,512]{1,0:T(8,128)(2,1)S(1)}, bf16[256,512]{1,0:T(8,128)(2,1)}, u32[]{:S(2)}) copy-start(bf16[256,512]{1,0:T(8,128)(2,1)} %aq.1) | copy-start | bytes 786436
  8.2 0.9 %copy-start.6 = (bf16[256,512]{1,0:T(8,128)(2,1)S(1)}, bf16[256,512]{1,0:T(8,128)(2,1)}, u32[]{:S(2)}) copy-start(bf16[256,512]{1,0:T(8,128)(2,1)} %ak.1) | copy-start | bytes 786436
  9.1 0.9 %copy-start.7 = (bf16[256,512]{1,0:T(8,128)(2,1)S(1)}, bf16[256,512]{1,0:T(8,128)(2,1)}, u32[]{:S(2)}) copy-start(bf16[256,512]{1,0:T(8,128)(2,1)} %av.1) | copy-start | bytes 786436
  10.1 0.7 copy-start.8

commit v2 on v1

--- a/solution.py
+++ b/solution.py
@@ -86,10 +86,11 @@
 def kernel(
     n,
     heads,
-    dq, dk, dv, gb, gate, gain, aq, ak, av, wd_any, wa_any,
+    dq_far, dk_far, dv_far, beta_far, rate_far, gate_far, gain_far, aq_far, ak_far, av_far, wd_far, wa_far,
     out,
+    dq, dk, dv, beta, rate, gate, gain, aq, ak, av, table,
     kv, own_out, carry, pair_own, pair_in, joined, s_in, s_out,
-    top, den, num, dh, ah, wd, wa, part_out, part_in, kept, sum_out, sum_in,
+    top, num, dh, ah, wd, wa, part_out, part_in, kept, sum_out, sum_in,
     w_sem, kv_send, kv_recv, pair_sem, s_sem, part_sem, sum_sem,
 ):
     c = lax.axis_index("ctx")
@@ -105,8 +106,13 @@
     rows = dq.shape[0]
 
     loads = [
-        pltpu.make_async_copy(wd_any, wd, w_sem.at[0]),
-        pltpu.make_async_copy(wa_any, wa, w_sem.at[1]),
+        pltpu.make_async_copy(far, near, w_sem.at[at])
+        for at, (far, near) in enumerate(
+            (
+                (beta_far, beta), (rate_far, rate), (dk_far, dk), (dq_far, dq), (dv_far, dv), (aq_far, aq),
+                (ak_far, ak), (av_far, av), (gate_far, gate), (gain_far, gain), (wa_far, wa), (wd_far, wd),
+            )
+        )
     ]
     for load in loads:
         load.start()
@@ -137,37 +143,44 @@
         )
 
     mine = (ak, av)
+    mine_far = (ak_far, av_far)
 
     def routes(part):
         return [
-            (has_up, lambda: kv_copy(0, part, mine[part], 2, above)),
-            (even == 1, lambda: kv_copy(1, part, mine[part], 1, partner)),
+            (has_up, lambda: kv_copy(0, part, mine_far[part], 2, above)),
+            (even == 1, lambda: kv_copy(1, part, mine_far[part], 1, partner)),
             (has_down & has_up, lambda: kv_copy(2, part, kv.at[1, part], 4, above)),
             (has_down & (even == 1), lambda: kv_copy(3, part, kv.at[1, part], 3, partner)),
             (has_down & (odd == 1), lambda: kv_copy(3, part, kv.at[1, part], 1, partner)),
             ((c >= 4) & (odd == 1), lambda: kv_copy(4, part, kv.at[3, part], 3, partner)),
         ]
 
-    def start(which):
-        for part in (0, 1):
-            for item in which:
-                condition, copy = routes(part)[item]
-
-                @pl.when(condition)
-                def _():
-                    copy().start()
+    def start(which, part):
+        for item in which:
+            condition, copy = routes(part)[item]
+
+            @pl.when(condition)
+            def _():
+                copy().start()
 
     def arrived(back, part):
-        kv_copy(0, part, mine[part], back, above).wait_recv()
-
-    start((0, 1))
+        kv_copy(0, part, mine_far[part], back, above).wait_recv()
+
+    for part in (0, 1):
+        start((0, 1), part)
 
     i, j = grids(rows)
-    summed = lax.dot_general(
-        jnp.where(i >= j, 1.0, 0.0), gb[...], (((1,), (0,)), ((), ())),
+    for load in loads[:5]:
+        load.wait()
+    table[...] = jnp.zeros_like(table)
+    table[0:heads, :] = beta[...]
+    table[8 : 8 + heads, :] = rate[...]
+    lines = lax.dot_general(
+        table[8:16, :], jnp.where(j >= i, 1.0, 0.0), (((1,), (0,)), ((), ())),
         precision=lax.Precision.HIGHEST, preferred_element_type=F32,
     )
-    turned = summed.T
+    table[8:16, :] = lines
+    turned = table[...].T
 
     def cut(ref, head):
         return ref[:, head * DH : (head + 1) * DH]
@@ -177,9 +190,9 @@
             [cut(dq, x) for x in some],
             [cut(dk, x) for x in some],
             [cut(dv, x) for x in some],
-            [gb[:, x : x + 1] for x in some],
-            [summed[:, heads + x : heads + x + 1] for x in some],
-            [turned[heads + x : heads + x + 1, :] for x in some],
+            [turned[:, x : x + 1] for x in some],
+            [turned[:, 8 + x : 9 + x] for x in some],
+            [lines[x : x + 1, :] for x in some],
         )
         for at, x in enumerate(some):
             pair_own[x, :, :DH] = moves[at].astype(BF16)
@@ -190,38 +203,44 @@
     pair_copy = remote(pair_own, pair_in, pair_sem.at[0], pair_sem.at[1], {"ctx": partner})
     pair_copy.start()
 
-    @pl.when(has_down)
-    def _():
-        for part in (0, 1):
+    for part in (0, 1):
+
+        @pl.when(has_down)
+        def _():
             arrived(2, part)
 
-    start((2, 3, 4))
+        start((2, 3, 4), part)
+
+    unit = DH ** (-0.5) * 1.4426950408889634
+    ones = jnp.ones((rows, DH), BF16)
 
     def attend(back):
         keys, vals = mine if back == 0 else (kv.at[back - 1, 0], kv.at[back - 1, 1])
-        for x in range(heads):
-            scores = mm(cut(aq, x), keys[:, x * DH : (x + 1) * DH], ((1,), (1,))) * DH ** (-0.5)
-            if back == 0:
-                scores = jnp.where(i >= j, scores, -1e30)
-            if back == WINDOW // rows:
-                scores = jnp.where(j > i, scores, -1e30)
-            block_top = jnp.max(scores, axis=-1, keepdims=True)
-            if back == 0:
-                high = block_top
-            else:
-                before = top[x][:, :1]
-                high = jnp.maximum(before, block_top)
-            weights = jnp.exp(scores - high)
-            block_den = jnp.sum(weights, axis=-1, keepdims=True)
-            block_num = mm(weights, vals[:, x * DH : (x + 1) * DH])
-            if back > 0:
-                factor = jnp.exp(before - high)
-                block_den = block_den + factor * den[x][:, :1]
-                block_num = block_num + factor * num[x]
-            top[x] = jnp.broadcast_to(high, (rows, DH))
-            den[x] = jnp.broadcast_to(block_den, (rows, DH))
-            num[x] = block_num
-
+        each = range(heads)
+        scores = [mm(cut(aq, x), keys[:, x * DH : (x + 1) * DH], ((1,), (1,))) for x in each]
+        if back == 0:
+            scores = [jnp.where(i >= j, s, -1e30) for s in scores]
+        if back == WINDOW // rows:
+            scores = [jnp.where(j > i, s, -1e30) for s in scores]
+        high = [jnp.max(s, axis=-1, keepdims=True) for s in scores]
+        if back > 0:
+            before = [top[x] for x in each]
+            sums = [num[x] for x in each]
+            high = [jnp.maximum(b[:, :1], m) for b, m in zip(before, high)]
+        weights = [jnp.exp2((s - m) * unit).astype(BF16) for s, m in zip(scores, high)]
+        added = [
+            mm(w, jnp.concatenate([vals[:, x * DH : (x + 1) * DH], ones], axis=1))
+            for x, w in zip(each, weights)
+        ]
+        if back > 0:
+            factor = [jnp.exp2((b[:, :1] - m) * unit) for b, m in zip(before, high)]
+            added = [n + f * o for n, f, o in zip(added, factor, sums)]
+        for x in each:
+            top[x] = jnp.broadcast_to(high[x], (rows, DH))
+            num[x] = added[x]
+
+    for load in loads[5:8]:
+        load.wait()
     attend(0)
 
     pair_copy.wait_recv()
@@ -239,15 +258,18 @@
     def _():
         s_in[...] = jnp.zeros_like(s_in)
 
-    @pl.when(has_up)
+    def pass_state_up():
+        for x in range(heads):
+            s_out[x] = (mm(joined[x, :, :DH], s_in[x]) + joined[x, :, DH:]).astype(BF16)
+        state_copy.start()
+
+    @pl.when(has_up & (c < 4))
     def _():
         @pl.when(has_down)
         def _():
             state_copy.wait_recv()
 
-        for x in range(heads):
-            s_out[x] = (mm(joined[x, :, :DH], s_in[x]) + joined[x, :, DH:]).astype(BF16)
-        state_copy.start()
+        pass_state_up()
 
     @pl.when(has_down)
     def _():
@@ -259,12 +281,18 @@
             arrived(1, part)
         attend(1)
 
-    @pl.when(c >= 4)
-    def _():
-        for part in (0, 1):
+    for part in (0, 1):
+
+        @pl.when(c >= 4)
+        def _():
             arrived(4, part)
 
-    start((5,))
+        start((5,), part)
+
+    @pl.when(has_up & (c >= 4))
+    def _():
+        state_copy.wait_recv()
+        pass_state_up()
 
     @pl.when(c >= 4)
     def _():
@@ -277,12 +305,14 @@
         attend(3)
 
     for x in range(heads):
-        ah[:, x * DH : (x + 1) * DH] = (num[x] / den[x]).astype(BF16)
+        ah[:, x * DH : (x + 1) * DH] = (num[x, :, :DH] / num[x, :, DH:]).astype(BF16)
 
     @pl.when(has_down & (above >= n))
     def _():
         state_copy.wait_recv()
 
+    for load in loads[8:]:
+        load.wait()
     for x in range(heads):
         state = s_in[x].astype(F32)
         its_pair = pair_in[x].astype(F32)
@@ -294,35 +324,51 @@
         normed = raw * scale * gain[...] * (gates / (1.0 + jnp.exp(-gates)))
         dh[:, x * DH : (x + 1) * DH] = normed.astype(BF16)
 
-    for load in loads:
-        load.wait()
     quarter = rows // 4
     width = out.shape[1]
     tile = 512
 
-    def project(targets, store):
+    half = width // 2
+
+    def project(targets, store, side):
         ds = [pl.ds(pl.multiple_of(t * quarter, quarter), quarter) for t in targets]
         d_rows = jnp.concatenate([dh[d, :] for d in ds], axis=0)
         a_rows = jnp.concatenate([ah[d, :] for d in ds], axis=0)
-        for low in range(0, width, tile):
-            part = mm(d_rows, wd[:, low : low + tile]) + mm(a_rows, wa[:, low : low + tile])
+        for low in range(0, half, tile):
+            at_col = side * half + low
+            part = mm(d_rows, wd[:, at_col : at_col + tile]) + mm(a_rows, wa[:, at_col : at_col + tile])
             for at in range(2):
-                store[at, :, low : low + tile] = part[at * quarter : (at + 1) * quarter].astype(BF16)
-
-    project((sibling, diagonal), part_out)
-    part_copy = remote(part_out, part_in, part_sem.at[0], part_sem.at[1], {"head": sibling})
-    part_copy.start()
-    project((h, across), kept)
-    part_copy.wait_recv()
-    sum_out[...] = (kept[1].astype(F32) + part_in[1].astype(F32)).astype(BF16)
-    sum_copy = remote(sum_out, sum_in, sum_sem.at[0], sum_sem.at[1], {"head": across})
-    sum_copy.start()
-    kept_sum = kept[0].astype(F32) + part_in[0].astype(F32)
-    sum_copy.wait_recv()
-    out[...] = (kept_sum + sum_in[...].astype(F32)).astype(BF16)
-
-    part_copy.wait_send()
-    sum_copy.wait_send()
+                store[side, at, :, low : low + tile] = part[at * quarter : (at + 1) * quarter].astype(BF16)
+
+    part_copies = [
+        remote(part_out.at[side], part_in.at[side], part_sem.at[0, side], part_sem.at[1, side], {"head": sibling})
+        for side in (0, 1)
+    ]
+    sum_copies = [
+        remote(sum_out.at[side], sum_in.at[side], sum_sem.at[0, side], sum_sem.at[1, side], {"head": across})
+        for side in (0, 1)
+    ]
+
+    def pass_across(side):
+        part_copies[side].wait_recv()
+        sum_out[side] = (kept[side, 1].astype(F32) + part_in[side, 1].astype(F32)).astype(BF16)
+        sum_copies[side].start()
+
+    project((sibling, diagonal), part_out, 0)
+    part_copies[0].start()
+    project((h, across), kept, 0)
+    project((sibling, diagonal), part_out, 1)
+    part_copies[1].start()
+    pass_across(0)
+    project((h, across), kept, 1)
+    pass_across(1)
+    for side in (0, 1):
+        kept_sum = kept[side, 0].astype(F32) + part_in[side, 0].astype(F32)
+        sum_copies[side].wait_recv()
+        out[:, side * half : (side + 1) * half] = (kept_sum + sum_in[side].astype(F32)).astype(BF16)
+
+    for copy in part_copies + sum_copies:
+        copy.wait_send()
     pair_copy.wait_send()
 
     @pl.when(has_up)
@@ -345,18 +391,20 @@
     rows, columns = delta_q.shape
     heads = columns // DH
     width = w_delta_out.shape[1]
-    gb = jnp.concatenate(
-        [beta, log_decay, jnp.zeros((rows, DH - 2 * heads), F32)], axis=1
-    )
     vmem = pl.BlockSpec(memory_space=pltpu.VMEM)
-    hbm = pl.BlockSpec(memory_space=pl.ANY)
+    hbm = pl.BlockSpec(memory_space=pltpu.HBM)
     quarter = rows // 4
     return pl.pallas_call(
         functools.partial(kernel, n, heads),
         out_shape=jax.ShapeDtypeStruct((quarter, width), BF16),
-        in_specs=[vmem] * 9 + [hbm] * 2,
+        in_specs=[hbm] * 12,
         out_specs=vmem,
-        scratch_shapes=[
+        scratch_shapes=[pltpu.VMEM((rows, columns), BF16)] * 3
+        + [pltpu.VMEM((heads, rows), F32)] * 2
+        + [pltpu.VMEM((rows, columns), BF16), pltpu.VMEM((1, DH), F32)]
+        + [pltpu.VMEM((rows, columns), BF16)] * 3
+        + [
+            pltpu.VMEM((DH, rows), F32),
             pltpu.VMEM((4, 2, rows, columns), BF16),
             pltpu.VMEM((heads, rows, DH), F32),
             pltpu.VMEM((heads, rows, DH), BF16),
@@ -366,31 +414,30 @@
             pltpu.VMEM((heads, DH, DH), BF16),
             pltpu.VMEM((heads, DH, DH), BF16),
             pltpu.VMEM((heads, rows, DH), F32),
-            pltpu.VMEM((heads, rows, DH), F32),
-            pltpu.VMEM((heads, rows, DH), F32),
+            pltpu.VMEM((heads, rows, 2 * DH), F32),
             pltpu.VMEM((rows, columns), BF16),
             pltpu.VMEM((rows, columns), BF16),
             pltpu.VMEM(w_delta_out.shape, BF16),
             pltpu.VMEM(w_attn_out.shape, BF16),
-            pltpu.VMEM((2, quarter, width), BF16),
-            pltpu.VMEM((2, quarter, width), BF16),
-            pltpu.VMEM((2, quarter, width), BF16),
-            pltpu.VMEM((quarter, width), BF16),
-            pltpu.VMEM((quarter, width), BF16),
-            pltpu.SemaphoreType.DMA((2,)),
+            pltpu.VMEM((2, 2, quarter, width // 2), BF16),
+            pltpu.VMEM((2, 2, quarter, width // 2), BF16),
+            pltpu.VMEM((2, 2, quarter, width // 2), BF16),
+            pltpu.VMEM((2, quarter, width // 2), BF16),
+            pltpu.VMEM((2, quarter, width // 2), BF16),
+            pltpu.SemaphoreType.DMA((12,)),
             pltpu.SemaphoreType.DMA((5, 2)),
             pltpu.SemaphoreType.DMA((4, 2)),
             pltpu.SemaphoreType.DMA((2,)),
             pltpu.SemaphoreType.DMA((2,)),
-            pltpu.SemaphoreType.DMA((2,)),
-            pltpu.SemaphoreType.DMA((2,)),
+            pltpu.SemaphoreType.DMA((2, 2)),
+            pltpu.SemaphoreType.DMA((2, 2)),
         ],
         compiler_params=pltpu.CompilerParams(
-            collective_id=0, has_side_effects=True, vmem_limit_bytes=48 * 1024 * 1024
+            collective_id=0, has_side_effects=True, vmem_limit_bytes=63 * 1024 * 1024
         ),
         cost_estimate=pl.CostEstimate(flops=4_000_000_000, bytes_accessed=8_000_000, transcendentals=2_000_000),
     )(
-        delta_q, delta_k, delta_v, gb, out_gate, norm_gain.reshape(1, DH),
+        delta_q, delta_k, delta_v, beta.T, log_decay.T, out_gate, norm_gain.reshape(1, DH),
         attn_q, attn_k, attn_v, w_delta_out, w_attn_out,
     )
 

time: 71.6 us -> 51.4 us (0.72)
  Pallas kernels: 59.7 us -> 49.6 us
  local copies, waits for them, and re-layouts: 11.3 us -> 1.67 us
    pallas_call x1, Pallas kernels: 59.7 us -> 49.6 us  [shards(): pl.pallas_call(functools.partial(kernel, n, heads), out_shape=jax.ShapeDt...]
    unnamed x21 -> x1, local copies, waits for them, and re-layouts: 11.2 us -> 1.67 us
where the time goes in v2:
time: 51.4 us; the launch traced here: 51.2 us
  Pallas kernels  49.6 us (96%)
  local copies, waits for them, and re-layouts  1.67 us (3%)
    pallas_call x1, Pallas kernels, shards(): pl.pallas_call(functools.partial(kernel, n, heads), out_shape=jax.ShapeDt...  49.6 us
    unnamed x1, local copies, waits for them, and re-layouts  1.67 us

profile of v2, /device:TPU:17, one launch (start us, length us, event | category | flops | bytes accessed | tf_op | source)
XLA Modules:
  0.0 51.2 jit_solution(6185334584908878199)
XLA Ops:
  0.0 49.6 %shard_map.118 = bf16[64,2048]{1,0:T(8,128)(2,1)} custom-call(bf16[256,512]{1,0:T(8,128)(2,1)} %dq_far.1, bf16[256,512]{1,0:T(8,128)(2,1)} %dk_far.1, bf16[256,512]{1,0:T(8,128)(2,1)} %dv_far.1, f32[4,256]{1,0:T(4,128)} %bitcast.3, f32[4,256]{1,0:T(4,128)} %bitcast.4, bf16[256,512]{1,0:T(8,128)(2,1)} %gate_far.1, f32[1,128]{1,0:T(1,128)} %bitcast.5, ...), custom_call_target="tpu_custom_call" | custom-call | flops 4000000000 | bytes 8000000 | tf_op jit(solution)/shard_map/pallas_call | solution.py:397
  49.6 1.7 %copy.14 = bf16[64,2048]{1,0:T(8,128)(2,1)} copy(bf16[64,2048]{1,0:T(8,128)(2,1)} %shard_map.118) | data formatting | bytes 524288

commit v3 on v2

--- a/solution.py
+++ b/solution.py
@@ -185,7 +185,7 @@
     def cut(ref, head):
         return ref[:, head * DH : (head + 1) * DH]
 
-    for some in ([0, 1], [2, 3]):
+    for part, some in enumerate((range(heads // 2), range(heads // 2, heads))):
         moves, adds, own, carries = delta_local(
             [cut(dq, x) for x in some],
             [cut(dk, x) for x in some],
@@ -200,16 +200,14 @@
             own_out[x] = own[at]
             carry[x] = carries[at].astype(BF16)
 
-    pair_copy = remote(pair_own, pair_in, pair_sem.at[0], pair_sem.at[1], {"ctx": partner})
-    pair_copy.start()
-
-    for part in (0, 1):
-
         @pl.when(has_down)
         def _():
             arrived(2, part)
 
         start((2, 3, 4), part)
+
+    pair_copy = remote(pair_own, pair_in, pair_sem.at[0], pair_sem.at[1], {"ctx": partner})
+    pair_copy.start()
 
     unit = DH ** (-0.5) * 1.4426950408889634
     ones = jnp.ones((rows, DH), BF16)
@@ -298,15 +296,6 @@
     def _():
         attend(4)
 
-    @pl.when(c >= 3)
-    def _():
-        for part in (0, 1):
-            arrived(3, part)
-        attend(3)
-
-    for x in range(heads):
-        ah[:, x * DH : (x + 1) * DH] = (num[x, :, :DH] / num[x, :, DH:]).astype(BF16)
-
     @pl.when(has_down & (above >= n))
     def _():
         state_copy.wait_recv()
@@ -323,6 +312,15 @@
         scale = lax.rsqrt(jnp.mean(raw * raw, axis=-1, keepdims=True) + 1e-06)
         normed = raw * scale * gain[...] * (gates / (1.0 + jnp.exp(-gates)))
         dh[:, x * DH : (x + 1) * DH] = normed.astype(BF16)
+
+    @pl.when(c >= 3)
+    def _():
+        for part in (0, 1):
+            arrived(3, part)
+        attend(3)
+
+    for x in range(heads):
+        ah[:, x * DH : (x + 1) * DH] = (num[x, :, :DH] / num[x, :, DH:]).astype(BF16)
 
     quarter = rows // 4
     width = out.shape[1]

time: 51.4 us -> 59.8 us (1.16)
  Pallas kernels: 49.6 us -> 58 us
    pallas_call x1, Pallas kernels: 49.6 us -> 58 us  [shards(): pl.pallas_call(functools.partial(kernel, n, heads), out_shape=jax.ShapeDt...]
where the time goes in v3:
time: 59.8 us; the launch traced here: 59.6 us
  Pallas kernels  58 us (97%)
  local copies, waits for them, and re-layouts  1.67 us (3%)
    pallas_call x1, Pallas kernels, shards(): pl.pallas_call(functools.partial(kernel, n, heads), out_shape=jax.ShapeDt...  58 us
    unnamed x1, local copies, waits for them, and re-layouts  1.67 us

profile of v3, /device:TPU:17, one launch (start us, length us, event | category | flops | bytes accessed | tf_op | source)
XLA Modules:
  0.0 59.6 jit_solution(10109423119793833275)
XLA Ops:
  0.0 58.0 %shard_map.118 = bf16[64,2048]{1,0:T(8,128)(2,1)} custom-call(bf16[256,512]{1,0:T(8,128)(2,1)} %dq_far.1, bf16[256,512]{1,0:T(8,128)(2,1)} %dk_far.1, bf16[256,512]{1,0:T(8,128)(2,1)} %dv_far.1, f32[4,256]{1,0:T(4,128)} %bitcast.3, f32[4,256]{1,0:T(4,128)} %bitcast.4, bf16[256,512]{1,0:T(8,128)(2,1)} %gate_far.1, f32[1,128]{1,0:T(1,128)} %bitcast.5, ...), custom_call_target="tpu_custom_call" | custom-call | flops 4000000000 | bytes 8000000 | tf_op jit(solution)/shard_map/pallas_call | solution.py:395
  58.0 1.7 %copy.14 = bf16[64,2048]{1,0:T(8,128)(2,1)} copy(bf16[64,2048]{1,0:T(8,128)(2,1)} %shard_map.118) | data formatting | bytes 524288
